TPU v7x, 32 devices: a whole 2x2x4 slice. The times are simulated.
32 devices in a mesh: beam: 2 (over y), chan: 4 (over z), tile: 2 (over x), pol: 2 (over core).
Axes of the slice: x: 2, y: 2, z: 4, core: 2. Of those that a mesh axis runs over, the one named last changes fastest.
Arguments:
- voltages: bfloat16 [8, 32, 100000], P(('beam', 'tile', 'pol'), 'chan'), parts along dimension 0, may hold values from -6 to 6
- flagged: int32 [4, 32], P(('tile', 'pol'), 'chan'), may hold values 0 or 1
- channel_table: int32 [4], replicated, may hold values from 0 to 3, each once
Outputs:
- visibilities: float32 [2, 8, 128, 128], P(None, ('beam', 'chan'), ('tile', 'pol')), parts along dimension 1
There are 2 independent parts, one for each index of `beam`. A program takes and returns all parts, laid end to end along the dimension named above; an argument that names none is the same for every part. Nothing has to cross between parts.
Inputs may be any that keep to these rules, and one draw needn't show every extreme that they name: `flagged`: 1 marks an input whose spectra are zeroed. `channel_table`: a permutation of the 4 channel blocks.
All inputs are finite; a program needn't handle non-finite values. No bound on the sum of `flagged` on one device may be relied on, other than what follows from the above.
Results may differ from a plain program's by a relative error of at most 0.0012.
Values may be sent and summed in bfloat16 or wider, within the bound.
A program may use at most 64 MiB of HBM per device.

v0:
```python
import math
import jax
import jax.numpy as jnp
import numpy as np
from jax import lax
from jax.sharding import PartitionSpec as P

N_OUTER = 160
N_INNER = 125
TAPS = 4
FRAMES = 2


def window_table(tap_count, frame_len):
    position = np.arange(tap_count * frame_len) * 1.0
    centre = (position - tap_count * frame_len / 2.0 + 0.5) / frame_len
    shaped = np.sin(np.pi * centre) / (np.pi * centre)
    prototype = shaped * (
        0.5 - 0.5 * np.cos(2.0 * np.pi * (position + 0.5) / (tap_count * frame_len))
    )
    prototype = prototype / np.sqrt(np.sum(prototype * prototype) / frame_len)
    return prototype.reshape(tap_count, frame_len)


def make_spectra(samples_in, flags_in, channel_table, n_chan):
    in_dev = samples_in.shape[0]
    frame_len = N_OUTER * N_INNER
    half_len = N_OUTER // 2
    filt = jnp.asarray(window_table(TAPS, frame_len), jnp.float32)
    frames_all = samples_in.astype(jnp.float32).reshape(in_dev, FRAMES + TAPS - 1, frame_len)
    filtered = jnp.zeros((in_dev, FRAMES, frame_len), jnp.float32)
    for tap_index in range(TAPS):
        filtered = filtered + filt[tap_index] * frames_all[:, tap_index : tap_index + FRAMES]
    filtered = filtered.reshape(in_dev, FRAMES, N_INNER, N_OUTER)
    inner_idx = jnp.arange(N_INNER, dtype=jnp.int32)
    inner_ang = (
        2.0
        * math.pi
        / N_INNER
        * (inner_idx[:, None] * inner_idx[None, :] % N_INNER).astype(jnp.float32)
    )
    inner_mat = jnp.concatenate([jnp.cos(inner_ang), -jnp.sin(inner_ang)], axis=0)
    section_one = jnp.einsum("kn,vsnm->vskm", inner_mat, filtered, precision=lax.Precision.HIGH)
    real_one = section_one[:, :, :N_INNER]
    imag_one = section_one[:, :, N_INNER:]
    outer_idx = jnp.arange(N_OUTER, dtype=jnp.int32)
    twist_ang = (
        2.0
        * math.pi
        / frame_len
        * (inner_idx[:, None] * outer_idx[None, :] % frame_len).astype(jnp.float32)
    )
    twist_cos = jnp.cos(twist_ang)
    twist_sin = jnp.sin(twist_ang)
    real_two = real_one * twist_cos + imag_one * twist_sin
    imag_two = imag_one * twist_cos - real_one * twist_sin
    joined = jnp.concatenate([real_two, imag_two], axis=3)
    block_width = half_len // n_chan
    out_pos = jnp.arange(half_len, dtype=jnp.int32)
    owner = out_pos // block_width
    onehot = owner[:, None] == jnp.arange(n_chan, dtype=jnp.int32)[None, :]
    chosen = jnp.sum(jnp.where(onehot, channel_table[None, :], 0), axis=1)
    outer_k = chosen * block_width + out_pos % block_width
    outer_ang = (
        2.0
        * math.pi
        / N_OUTER
        * (outer_k[:, None] * outer_idx[None, :] % N_OUTER).astype(jnp.float32)
    )
    outer_cos = jnp.cos(outer_ang)
    outer_sin = jnp.sin(outer_ang)
    real_rows = jnp.concatenate([outer_cos, outer_sin], axis=1)
    imag_rows = jnp.concatenate([-outer_sin, outer_cos], axis=1)
    outer_mat = jnp.stack([real_rows, imag_rows], axis=0)
    spectrum = jnp.einsum("vskn,rjn->vrsjk", joined, outer_mat, precision=lax.Precision.HIGH)
    spectrum = spectrum.reshape(in_dev, 2, FRAMES, half_len * N_INNER)
    kept_mask = (1 - flags_in).astype(jnp.float32)
    spectrum = spectrum * (kept_mask[:, None, None, None] / math.sqrt(frame_len))
    return spectrum.astype(jnp.bfloat16)


def correlate(left_rows, panel_cols, scale):
    return (
        jnp.einsum("rik,jk->rij", left_rows, panel_cols, preferred_element_type=jnp.float32) * scale
    )


def on_device(voltages, flagged, channel_table):
    n_chan = lax.axis_size("chan")
    spectra = make_spectra(voltages[0], flagged[0], channel_table, n_chan)
    turned = lax.all_to_all(spectra, "chan", split_axis=3, concat_axis=0, tiled=True)
    group_len = turned.shape[0]
    chb_len = turned.shape[3]
    half_k = FRAMES * chb_len
    scale = 1.0 / math.sqrt(FRAMES * chb_len)
    band_rows = turned.reshape(group_len, 2 * half_k)
    swapped = jnp.concatenate([band_rows[:, half_k:], -band_rows[:, :half_k]], axis=1)
    left_rows = jnp.stack([band_rows, swapped], axis=0)
    vis_local = correlate(
        left_rows, lax.all_gather(band_rows, ("tile", "pol"), axis=0, tiled=True), scale
    )
    return vis_local[:, None]


def solution(mesh):
    in_specs = (P(("beam", "tile", "pol"), "chan", None), P(("tile", "pol"), "chan"), P())
    out_specs = P(None, ("beam", "chan"), ("tile", "pol"), None)
    return jax.shard_map(
        on_device, mesh=mesh, in_specs=in_specs, out_specs=out_specs, check_vma=False
    )
```

profile of v0, /device:TPU:0, one launch (start us, length us, event | category | flops | bytes accessed | tf_op | source)
XLA Modules:
  0.0 155.5 jit_solution(12879074996876843924)
XLA Ops:
  6.5 0.0 all-gather.2.cloned.1.call-start
  6.5 0.9 sine_negate_fusion
  7.5 1.0 fusion.38
  8.5 0.7 multiply_bitcast_fusion
  9.2 0.7 select_reduce_fusion
  9.9 1.1 fusion.42
  11.0 5.3 %reshape.90 = f32[8,5,20000]{2,1,0:T(8,128)} reshape(bf16[1,8,100000]{2,1,0:T(8,128)(2,1)} %param.4) | data formatting | bytes 4800000 | tf_op jit(solution)/shard_map/convert_element_type | solution.py:30
  16.3 0.0 copy-start.3
  16.3 0.0 copy-start.4
  16.3 0.0 copy-start.5
  16.3 0.0 copy-start.6
  16.3 10.0 %fusion.57 = (f32[8,2,20000]{2,1,0:T(2,128)S(1)}, f32[8,2,20000]{2,1,0:T(2,128)S(1)}, f32[8,2,20000]{2,1,0:T(2,128)S(1)}, f32[8,2,20000]{2,1,0:T(2,128)S(1)}) fusion(f32[8,5,20000]{2,1,0:T(8,128)} %reshape.90), kind=kLoop, calls=%fused_computation.76 | loop fusion | bytes 10240000 | tf_op jit(solution)/shard_map/slice | solution.py:33
  26.4 0.0 copy-done.3
  26.4 0.0 copy-done.4
  26.4 0.0 copy-done.5
  26.4 0.0 copy-done.6
  26.4 0.5 fusion.15
  26.9 1.3 reshape.87
  28.2 1.1 maximum_bitcast_fusion.9
  29.3 0.0 copy-start.1
  29.3 0.0 copy-start.2
  29.3 2.8 %fusion.7 = f32[8,2,250,160]{2,3,1,0:T(8,128)S(1)} fusion(f32[8,2,125,160]{3,2,0,1:T(8,128)S(1)} %reshape.87, f32[125,125]{1,0:T(8,128)} %get-tuple-element.18, f32[125,125]{1,0:T(8,128)} %get-tuple-element.19), kind=kOutput, calls=%fused_computation.8 | convolution fusion | flops 480031232 | bytes 3965000 | tf_op jit(solution)/shard_map/kn,vsnm->vskm/dot_general | solution.py:43
  32.1 0.0 copy-done.1
  32.1 0.0 copy-done.2
  32.1 0.7 multiply_add_fusion
  32.8 1.2 fusion.10
  34.1 1.7 %reshape.95 = f32[8,2,2,10000]{3,2,0,1:T(2,128)S(1)} reshape(f32[8,2,2,80,125]{4,3,2,0,1:T(8,128)S(1)} %fusion.10) | data formatting | bytes 2560000 | tf_op jit(solution)/shard_map/reshape | solution.py:76
  35.7 0.1 fusion.14
  35.9 16.1 %copy.32 = bf16[8,2,2,10000]{0,2,1,3:T(2,128)(2,1)} copy(bf16[8,2,2,10000]{3,0,2,1:T(8,128)(2,1)S(1)} %fusion.14) | data formatting | bytes 1280000 | tf_op jit(solution)/shard_map/convert_element_type | solution.py:79
  52.0 13.1 %reshape.96 = bf16[4,2,40000]{2,1,0:T(2,128)(2,1)S(1)} reshape(bf16[10000,2,2,8]{3,2,1,0:T(2,128)(2,1)} %bitcast.48) | data formatting | bytes 1280000
  65.2 23.1 %all_to_all.15 = bf16[4,2,40000]{2,1,0:T(2,128)(2,1)S(1)} all-to-all(bf16[4,2,40000]{2,1,0:T(2,128)(2,1)S(1)} %reshape.96), channel_id=1, replica_groups=mesh['beam'=2,'chan'=4,'tile'=2,'pol'=2] {'chan'}, dimensions={0} | all-to-all | bytes 1280000 | tf_op jit(solution)/shard_map/all_to_all | solution.py:91
  88.3 11.1 %reshape.97 = bf16[10000,2,2,8]{3,2,1,0:T(2,128)(2,1)} reshape(bf16[4,2,40000]{2,1,0:T(2,128)(2,1)S(1)} %all_to_all.15) | data formatting | bytes 1280000
  99.3 19.7 %copy.33 = bf16[8,2,2,4,2500]{4,2,1,0,3:T(2,128)(2,1)S(1)} copy(bf16[8,2,2,4,2500]{0,2,1,4,3:T(2,128)(2,1)} %bitcast.49) | data formatting | bytes 1280000 | tf_op jit(solution)/shard_map/all_to_all | solution.py:91
  119.1 1.5 reshape.89
  120.6 0.0 copy-start
  120.6 0.0 all-gather.2.cloned.1.call-update
  120.6 0.7 stack_reshape.3
  121.4 0.3 copy-done
  121.7 0.2 fusion.58
  121.9 0.2 maximum_bitcast_fusion.4
  122.0 23.3 %all-gather.2.cloned.1.call-done = bf16[128,10000]{1,0:T(8,128)(2,1)} async-done(((bf16[32,10000]{1,0:T(8,128)(2,1)}), bf16[128,10000]{1,0:T(8,128)(2,1)}) %all-gather.2.cloned.1.call-update) | async-done | bytes 2560016 | tf_op jit(solution)/shard_map/all_gather | solution.py:100
  145.3 3.4 %fusion.23 = f32[2,1,32,128]{3,2,1,0:T(8,128)} fusion(bf16[128,10000]{1,0:T(8,128)(2,1)} %all-gather.2.cloned.1.call-done, bf16[1,32,10000]{2,1,0:T(8,128)(2,1)S(1)} %maximum_bitcast_fusion.4, bf16[1,32,10000]{2,1,0:T(8,128)(2,1)S(1)} %stack_reshape.3), kind=kOutput, calls=%fused_computation.25 | convolution fusion | flops 164488192 | bytes 3872768 | tf_op jit(solution)/shard_map/rik,jk->rij/dot_general | solution.py:84
  (2 shorter events, 0.0 us)
Async XLA Ops:
  6.5 138.7 %all-gather.2.cloned.1.call-start = ((), (), s32[]{:S(2)}) async-start(), calls=%async_computation.1 | async-start | bytes 3235840 | tf_op jit(solution)/shard_map/all_gather | solution.py:100
  16.3 10.1 %copy-start.3 = (f32[20000]{0:T(1024)S(1)}, f32[20000]{0:T(1024)}, u32[]{:S(2)}) copy-start(f32[20000]{0:T(1024)} %constant.79) | copy-start | bytes 240004
  16.3 10.1 %copy-start.4 = (f32[20000]{0:T(1024)S(1)}, f32[20000]{0:T(1024)}, u32[]{:S(2)}) copy-start(f32[20000]{0:T(1024)} %constant.77) | copy-start | bytes 240004
  16.3 10.1 %copy-start.5 = (f32[20000]{0:T(1024)S(1)}, f32[20000]{0:T(1024)}, u32[]{:S(2)}) copy-start(f32[20000]{0:T(1024)} %constant.75) | copy-start | bytes 240004
  16.3 10.1 %copy-start.6 = (f32[20000]{0:T(1024)S(1)}, f32[20000]{0:T(1024)}, u32[]{:S(2)}) copy-start(f32[20000]{0:T(1024)} %constant.73) | copy-start | bytes 240004
  29.3 2.8 %copy-start.1 = (f32[125,160]{0,1:T(8,128)S(1)}, f32[125,160]{0,1:T(8,128)}, u32[]{:S(2)}) copy-start(f32[125,160]{0,1:T(8,128)} %get-tuple-element.20) | copy-start | bytes 240004
  29.3 2.8 %copy-start.2 = (f32[125,160]{0,1:T(8,128)S(1)}, f32[125,160]{0,1:T(8,128)}, u32[]{:S(2)}) copy-start(f32[125,160]{0,1:T(8,128)} %get-tuple-element.21) | copy-start | bytes 240004
  120.6 1.1 copy-start
Sparse Core Ops, SparseCore 0:
  120.8 24.4 all-gather.1
where the time goes:
time: 156 us; the launch traced here: 155 us
  local copies, waits for them, and re-layouts  81 us (52%)
  waiting for transfers between devices  23.3 us (15%)
  blocking collectives  23.1 us (15%)
  between operations  13.5 us (9%)
  matrix products  7.41 us (5%)
  other arithmetic  7.17 us (5%)
    unnamed x16, local copies, waits for them, and re-layouts  24.6 us
    all_gather x1, waiting for transfers between devices, on_device(): lax.all_gather(band_rows, ('tile', 'pol'), axis=0, tiled=True)  23.3 us
    all_to_all x1, blocking collectives, on_device(): lax.all_to_all(spectra, 'chan', split_axis=3, concat_axis=0, tiled=True)  23.1 us
    all_to_all x1, local copies, waits for them, and re-layouts, on_device(): lax.all_to_all(spectra, 'chan', split_axis=3, concat_axis=0, tiled=True)  19.7 us
    convert_element_type x1, local copies, waits for them, and re-layouts, make_spectra(): return spectrum.astype(jnp.bfloat16)  16.1 us
    slice x1, local copies, waits for them, and re-layouts, make_spectra(): frames_all[:, tap_index:tap_index + FRAMES]  10 us
    convert_element_type x1, local copies, waits for them, and re-layouts, make_spectra(): samples_in.astype(jnp.float32).reshape(in_dev, FRAMES + TAPS - 1, frame_len)  5.31 us
    dot_general x1, matrix products, correlate(): jnp.einsum('rik,jk->rij', left_rows, panel_cols, preferred_element_type=j...  3.36 us
  transfers between devices with their start and end apart: 1, of which 1 were waited for; matrix products, arithmetic and copies ran while one was open for 1% of the time, Pallas kernels for 0%

commit v1 on v0

--- a/solution.py
+++ b/solution.py
@@ -1,3 +1,4 @@
+import functools
 import math
 import jax
 import jax.numpy as jnp
@@ -9,6 +10,27 @@
 N_INNER = 125
 TAPS = 4
 FRAMES = 2
+
+
+def launch_tokens_up(xx, axis_no):
+    after = list(xx.shape[1:])
+    after[axis_no] *= xx.shape[0]
+    return jnp.moveaxis(xx, 0, axis_no).reshape(after)
+
+
+def _convert_core(t0, a_name, k_dim):
+    n_slots = jax.lax.psum(1, a_name)
+    rows = tuple(((k, (k + 1) % n_slots) for k in range(n_slots)))
+    kept_rows = [t0]
+    while len(kept_rows) < n_slots:
+        kept_rows.append(jax.lax.ppermute(kept_rows[-1], a_name, perm=rows))
+    x_next = jax.lax.axis_index(a_name)
+    all_values = jnp.stack(kept_rows)
+    kept_rows = all_values[(x_next - jnp.arange(n_slots)) % n_slots]
+    return launch_tokens_up(kept_rows, k_dim)
+
+
+create_edges_for = functools.partial(_convert_core, a_name=("tile", "pol"), k_dim=0)
 
 
 def window_table(tap_count, frame_len):
@@ -96,9 +118,7 @@
     band_rows = turned.reshape(group_len, 2 * half_k)
     swapped = jnp.concatenate([band_rows[:, half_k:], -band_rows[:, :half_k]], axis=1)
     left_rows = jnp.stack([band_rows, swapped], axis=0)
-    vis_local = correlate(
-        left_rows, lax.all_gather(band_rows, ("tile", "pol"), axis=0, tiled=True), scale
-    )
+    vis_local = correlate(left_rows, create_edges_for(band_rows), scale)
     return vis_local[:, None]
 
 

time: 156 us -> 148 us (0.949)
  between operations: 13.5 us -> 0.2 us
  waiting for transfers between devices: 23.3 us -> 28.2 us
    ppermute x0 -> x3, waiting for transfers between devices: none -> 28.2 us  [_convert_core(): kept_rows.append(jax.lax.ppermute(kept_rows[-1], a_name, perm=rows))]
    all_gather x1 -> x0, waiting for transfers between devices: 23.3 us -> none  [on_device(): lax.all_gather(band_rows, ('tile', 'pol'), axis=0, tiled=True)]
    gather x0 -> x1, local copies, waits for them, and re-layouts: none -> 2.31 us  [_convert_core(): kept_rows = all_values[(x_next - jnp.arange(n_slots)) % n_slots]]
    unnamed x16 -> x14, local copies, waits for them, and re-layouts: 24.6 us -> 24.2 us
  transfers between devices with their start and end apart: 1 -> 3, of which waited for: 1 -> 3; matrix products, arithmetic and copies ran while one was open for 1% -> 1% of each run, Pallas kernels for 0% -> 0%
where the time goes in v1:
time: 148 us; the launch traced here: 147 us
  local copies, waits for them, and re-layouts  81.9 us (55%)
  waiting for transfers between devices  28.2 us (19%)
  blocking collectives  23.1 us (16%)
  matrix products  7.59 us (5%)
  other arithmetic  5.9 us (4%)
    ppermute x3, waiting for transfers between devices, _convert_core(): kept_rows.append(jax.lax.ppermute(kept_rows[-1], a_name, perm=rows))  28.2 us
    unnamed x14, local copies, waits for them, and re-layouts  24.2 us
    all_to_all x1, blocking collectives, on_device(): lax.all_to_all(spectra, 'chan', split_axis=3, concat_axis=0, tiled=True)  23.1 us
    all_to_all x1, local copies, waits for them, and re-layouts, on_device(): lax.all_to_all(spectra, 'chan', split_axis=3, concat_axis=0, tiled=True)  19.7 us
    convert_element_type x1, local copies, waits for them, and re-layouts, make_spectra(): return spectrum.astype(jnp.bfloat16)  16.2 us
    slice x1, local copies, waits for them, and re-layouts, make_spectra(): frames_all[:, tap_index:tap_index + FRAMES]  9.79 us
    convert_element_type x1, local copies, waits for them, and re-layouts, make_spectra(): samples_in.astype(jnp.float32).reshape(in_dev, FRAMES + TAPS - 1, frame_len)  5.31 us
    dot_general x1, matrix products, correlate(): jnp.einsum('rik,jk->rij', left_rows, panel_cols, preferred_element_type=j...  3.57 us
  transfers between devices with their start and end apart: 3, of which 3 were waited for; matrix products, arithmetic and copies ran while one was open for 1% of the time, Pallas kernels for 0%

profile of v1, /device:TPU:0, one launch (start us, length us, event | category | flops | bytes accessed | tf_op | source)
XLA Modules:
  0.0 146.9 jit_solution(12678527764755539859)
XLA Ops:
  0.0 0.9 sine_negate_fusion
  0.9 0.3 fusion.33
  1.3 5.3 %reshape.143 = f32[8,5,20000]{2,1,0:T(8,128)} reshape(bf16[1,8,100000]{2,1,0:T(8,128)(2,1)} %param.4) | data formatting | bytes 4800000 | tf_op jit(solution)/shard_map/convert_element_type | solution.py:52
  6.6 0.0 copy-start
  6.6 0.0 copy-start.1
  6.6 0.0 copy-start.2
  6.6 0.0 copy-start.3
  6.6 9.8 %fusion.54 = (f32[8,2,20000]{2,1,0:T(2,128)S(1)}, f32[8,2,20000]{2,1,0:T(2,128)S(1)}, f32[8,2,20000]{2,1,0:T(2,128)S(1)}, f32[8,2,20000]{2,1,0:T(2,128)S(1)}) fusion(f32[8,5,20000]{2,1,0:T(8,128)} %reshape.143), kind=kLoop, calls=%fused_computation.84 | loop fusion | bytes 10240000 | tf_op jit(solution)/shard_map/slice | solution.py:55
  16.4 0.0 copy-done
  16.4 0.0 copy-done.1
  16.4 0.0 copy-done.2
  16.5 0.0 copy-done.3
  16.5 0.5 fusion.14
  17.0 0.0 copy-start.4
  17.0 1.3 reshape.139
  18.3 0.0 copy-done.4
  18.3 0.1 select_reduce_fusion
  18.4 0.4 fusion.37
  18.8 2.8 %fusion.5 = f32[8,2,250,160]{2,3,1,0:T(8,128)S(1)} fusion(f32[8,2,125,160]{3,2,0,1:T(8,128)S(1)} %reshape.139, f32[125,125]{1,0:T(8,128)} %get-tuple-element.18, f32[125,125]{1,0:T(8,128)} %get-tuple-element.19), kind=kOutput, calls=%fused_computation.8 | convolution fusion | flops 480031232 | bytes 3965000 | tf_op jit(solution)/shard_map/kn,vsnm->vskm/dot_general | solution.py:65
  21.6 0.7 multiply_add_fusion
  22.3 0.1 maximum_bitcast_fusion.9
  22.4 1.3 fusion.8
  23.6 0.0 copy-start.5
  23.6 1.7 %reshape.156 = f32[8,2,2,10000]{3,2,0,1:T(2,128)S(1)} reshape(f32[8,2,2,80,125]{4,3,2,0,1:T(8,128)S(1)} %fusion.8) | data formatting | bytes 2560000 | tf_op jit(solution)/shard_map/reshape | solution.py:98
  25.3 0.0 copy-done.5
  25.3 0.1 fusion.13
  25.5 16.2 %copy.37 = bf16[8,2,2,10000]{0,2,1,3:T(2,128)(2,1)} copy(bf16[8,2,2,10000]{3,0,2,1:T(8,128)(2,1)S(1)} %fusion.13) | data formatting | bytes 1280000 | tf_op jit(solution)/shard_map/convert_element_type | solution.py:101
  41.6 13.1 %reshape.157 = bf16[4,2,40000]{2,1,0:T(2,128)(2,1)S(1)} reshape(bf16[10000,2,2,8]{3,2,1,0:T(2,128)(2,1)} %bitcast.50) | data formatting | bytes 1280000
  54.8 23.1 %all_to_all.15 = bf16[4,2,40000]{2,1,0:T(2,128)(2,1)S(1)} all-to-all(bf16[4,2,40000]{2,1,0:T(2,128)(2,1)S(1)} %reshape.157), channel_id=1, replica_groups=mesh['beam'=2,'chan'=4,'tile'=2,'pol'=2] {'chan'}, dimensions={0} | all-to-all | bytes 1280000 | tf_op jit(solution)/shard_map/all_to_all | solution.py:113
  77.9 11.1 %reshape.158 = bf16[10000,2,2,8]{3,2,1,0:T(2,128)(2,1)} reshape(bf16[4,2,40000]{2,1,0:T(2,128)(2,1)S(1)} %all_to_all.15) | data formatting | bytes 1280000
  89.0 19.7 %copy.38 = bf16[8,2,2,4,2500]{4,2,1,0,3:T(2,128)(2,1)S(1)} copy(bf16[8,2,2,4,2500]{0,2,1,4,3:T(2,128)(2,1)} %bitcast.51) | data formatting | bytes 1280000 | tf_op jit(solution)/shard_map/all_to_all | solution.py:113
  108.7 0.7 reshape.141
  109.4 0.1 collective-permute-start
  109.5 0.7 stack_reshape.4
  110.3 9.3 %collective-permute-done = bf16[32,10000]{1,0:T(8,128)(2,1)} collective-permute-done((bf16[32,10000]{1,0:T(8,128)(2,1)S(1)}, bf16[32,10000]{1,0:T(8,128)(2,1)}, u32[]{:S(2)}, u32[]{:S(2)}) %collective-permute-start) | collective-permute-done | bytes 640032 | tf_op jit(solution)/shard_map/ppermute | solution.py:26
  119.5 0.0 collective-permute-start.1
  119.5 0.2 fusion.55
  119.7 10.0 %collective-permute-done.1 = bf16[32,10000]{1,0:T(8,128)(2,1)S(1)} collective-permute-done((bf16[32,10000]{1,0:T(8,128)(2,1)}, bf16[32,10000]{1,0:T(8,128)(2,1)S(1)}, u32[]{:S(2)}, u32[]{:S(2)}) %collective-permute-start.1) | collective-permute-done | bytes 640032 | tf_op jit(solution)/shard_map/ppermute | solution.py:26
  129.6 0.0 collective-permute-start.2
  129.7 1.0 maximum_bitcast_fusion.4
  130.6 8.9 %collective-permute-done.2 = bf16[32,10000]{1,0:T(8,128)(2,1)S(1)} collective-permute-done((bf16[32,10000]{1,0:T(8,128)(2,1)S(1)}, bf16[32,10000]{1,0:T(8,128)(2,1)S(1)}, u32[]{:S(2)}, u32[]{:S(2)}) %collective-permute-start.2) | collective-permute-done | bytes 640032 | tf_op jit(solution)/shard_map/ppermute | solution.py:26
  139.6 1.5 %pad_maximum_fusion = bf16[4,32,10000]{2,1,0:T(8,128)(2,1)S(1)} fusion(bf16[1,32,10000]{2,1,0:T(8,128)(2,1)S(1)} %bitcast.56, bf16[1,32,10000]{2,1,0:T(8,128)(2,1)S(1)} %bitcast.55, bf16[1,32,10000]{2,1,0:T(8,128)(2,1)} %bitcast.13, bf16[1,32,10000]{2,1,0:T(8,128)(2,1)S(1)} %stack_reshape.4), kind=kLoop, calls=%fused_computation.5 | loop fusion | flops 3840000 | bytes 5120000 | tf_op jit(solution)/shard_map/stack | solution.py:28
  141.0 2.3 %gather_fusion = bf16[4,32,10000]{2,1,0:T(8,128)(2,1)} fusion(bf16[4,32,10000]{2,1,0:T(8,128)(2,1)S(1)} %pad_maximum_fusion, s32[1024]{0:T(1024)S(1)} %pad_clamp_fusion), kind=kCustom, calls=%fused_computation | custom fusion | bytes 5120016 | tf_op jit(solution)/shard_map/gather | solution.py:29
  143.4 3.6 %fusion.20 = f32[2,1,32,128]{3,2,1,0:T(8,128)} fusion(bf16[128,10000,1]{1,0,2:T(8,128)(2,1)} %bitcast.52, bf16[1,32,10000]{2,1,0:T(8,128)(2,1)} %maximum_bitcast_fusion.4, bf16[1,32,10000]{2,1,0:T(8,128)(2,1)S(1)} %stack_reshape.4), kind=kOutput, calls=%fused_computation.26 | convolution fusion | flops 164488192 | bytes 3872768 | tf_op jit(solution)/shard_map/rik,jk->rij/dot_general | solution.py:106
  (5 shorter events, 0.0 us)
Async XLA Ops:
  6.6 9.8 %copy-start = (f32[20000]{0:T(1024)S(1)}, f32[20000]{0:T(1024)}, u32[]{:S(2)}) copy-start(f32[20000]{0:T(1024)} %constant.101) | copy-start | bytes 240004
  6.6 9.8 %copy-start.1 = (f32[20000]{0:T(1024)S(1)}, f32[20000]{0:T(1024)}, u32[]{:S(2)}) copy-start(f32[20000]{0:T(1024)} %constant.103) | copy-start | bytes 240004
  6.6 9.8 %copy-start.2 = (f32[20000]{0:T(1024)S(1)}, f32[20000]{0:T(1024)}, u32[]{:S(2)}) copy-start(f32[20000]{0:T(1024)} %constant.97) | copy-start | bytes 240004
  6.6 9.8 %copy-start.3 = (f32[20000]{0:T(1024)S(1)}, f32[20000]{0:T(1024)}, u32[]{:S(2)}) copy-start(f32[20000]{0:T(1024)} %constant.99) | copy-start | bytes 240004
  17.0 1.3 copy-start.4
  23.6 1.7 %copy-start.5 = (s32[1,8]{1,0:T(1,128)S(1)}, s32[1,8]{1,0:T(1,128)}, u32[]{:S(2)}) copy-start(s32[1,8]{1,0:T(1,128)} %param.5) | copy-start | bytes 100
  109.4 10.1 %collective-permute-start = (bf16[32,10000]{1,0:T(8,128)(2,1)S(1)}, bf16[32,10000]{1,0:T(8,128)(2,1)}, u32[]{:S(2)}, u32[]{:S(2)}) collective-permute-start(bf16[32,10000]{1,0:T(8,128)(2,1)S(1)} %reshape.141), channel_id=1, source_target_pairs={{0,1},{1,2},{2,3},{3,0},{4,5},{5,6},{6,7},{7,4},{8,9},{9,10},{10,1... | collective-permute-start | bytes 1920008 | tf_op jit(solution)/shard_map/ppermute | solution.py:26
  119.5 10.1 %collective-permute-start.1 = (bf16[32,10000]{1,0:T(8,128)(2,1)}, bf16[32,10000]{1,0:T(8,128)(2,1)S(1)}, u32[]{:S(2)}, u32[]{:S(2)}) collective-permute-start(bf16[32,10000]{1,0:T(8,128)(2,1)} %collective-permute-done), channel_id=1, source_target_pairs={{0,1},{1,2},{2,3},{3,0},{4,5},{5,6},{6,7},{7,4},{8,9},{9,10},{10,1... | collective-permute-start | bytes 1920008 | tf_op jit(solution)/shard_map/ppermute | solution.py:26
  129.6 9.9 %collective-permute-start.2 = (bf16[32,10000]{1,0:T(8,128)(2,1)S(1)}, bf16[32,10000]{1,0:T(8,128)(2,1)S(1)}, u32[]{:S(2)}, u32[]{:S(2)}) collective-permute-start(bf16[32,10000]{1,0:T(8,128)(2,1)S(1)} %collective-permute-done.1), channel_id=1, source_target_pairs={{0,1},{1,2},{2,3},{3,0},{4,5},{5,6},{6,7},{7,4},{8,9},{9,10},{10,1... | collective-permute-start | bytes 1920008 | tf_op jit(solution)/shard_map/ppermute | solution.py:26
